TPU v7x, 512 devices: a whole 4x8x8 slice. The times are simulated.
512 devices in a mesh: gx: 8 (over x, core), gy: 8 (over z), gz: 8 (over y).
Axes of the slice: x: 4, y: 8, z: 8, core: 2. Of those that a mesh axis runs over, the one named last changes fastest.
Arguments:
- prior_basis: float32 [32, 128, 12288], P('gx', 'gy', 'gz'), may hold values from -6 to 6
- edge_weights: float32 [3, 32, 128, 128], P(None, 'gx', 'gy', 'gz'), may hold values from 0.5 to 1.5
- spectral_shift: float32 [1], replicated, may hold values from 0.5 to 4
Outputs:
- new_basis: float32 [32, 128, 16384], P('gx', 'gy', 'gz')
- projection: float32 [96, 128], replicated
- triangle: float32 [128, 128], replicated
All inputs are finite; a program needn't handle non-finite values.
Results may differ from a plain program's by a relative error of at most 0.002.
Values sent between devices are 32-bit elements; how exact they have to be, the bound alone decides.
A program may use at most 64 MiB of HBM per device.

v0:
```python
import jax
import jax.numpy as jnp
from jax import lax
from jax.sharding import PartitionSpec as P

BLOCK = 32
POWERS = 4
BASIS = 96
PRECISE = lax.Precision.HIGHEST
OPERATOR_SCALE = 11.0


def passed_along(block, axis, distance):
    devices = range(lax.axis_size(axis))
    route = [(i - distance, i) for i in devices if i - distance in devices]
    return lax.ppermute(block, axis, route)


def with_halo(block, sides, width):
    for axis, dim in sides:
        count = lax.axis_size(axis)
        forward = [(i, i + 1) for i in range(count - 1)]
        backward = [(target, source) for source, target in forward]
        low = lax.ppermute(
            lax.slice_in_dim(block, block.shape[dim] - width, None, axis=dim), axis, forward
        )
        high = lax.ppermute(lax.slice_in_dim(block, 0, width, axis=dim), axis, backward)
        block = jnp.concatenate([low, block, high], axis=dim)
    return block


def crop_margin(values, layers, columns):
    return values[
        ...,
        layers : values.shape[-3] - layers,
        layers : values.shape[-2] - layers,
        layers * columns : values.shape[-1] - layers * columns,
    ]


def stencil(padded, weight_pad, shift_value, columns):
    centre = crop_margin(padded, 1, columns)
    inner_weights = crop_margin(weight_pad, 1, columns)
    below_x = weight_pad[0, :-2, 1:-1, columns:-columns]
    below_y = weight_pad[1, 1:-1, :-2, columns:-columns]
    below_z = weight_pad[2, 1:-1, 1:-1, : -2 * columns]
    summed = inner_weights[0] * (centre - padded[2:, 1:-1, columns:-columns]) + below_x * (
        centre - padded[:-2, 1:-1, columns:-columns]
    )
    summed = (
        summed
        + inner_weights[1] * (centre - padded[1:-1, 2:, columns:-columns])
        + below_y * (centre - padded[1:-1, :-2, columns:-columns])
    )
    summed = (
        summed
        + inner_weights[2] * (centre - padded[1:-1, 1:-1, 2 * columns :])
        + below_z * (centre - padded[1:-1, 1:-1, : -2 * columns])
    )
    return (summed + shift_value * centre) / OPERATOR_SCALE - centre


def per_device(prior_basis, edge_weights, spectral_shift):
    size_x = prior_basis.shape[0]
    size_y = prior_basis.shape[1]
    size_z = prior_basis.shape[2] // BASIS
    cell_local = size_x * size_y * size_z
    cell_count = cell_local * lax.axis_size("gx") * lax.axis_size("gy") * lax.axis_size("gz")
    shift_value = spectral_shift[0]
    basis_rows = prior_basis.reshape(cell_local, BASIS)
    start_block = prior_basis.reshape(size_x, size_y, size_z, BASIS)[..., BASIS - BLOCK :]
    lower_x = passed_along(edge_weights[0, size_x - 1 :], "gx", 1)
    lower_y = passed_along(edge_weights[1, :, size_y - 1 :], "gy", 1)
    lower_z = passed_along(edge_weights[2, :, :, size_z - 1 :], "gz", 1)
    weight_pad = jnp.pad(edge_weights, ((0, 0), (1, 1), (1, 1), (1, 1)))
    weight_pad = weight_pad.at[0, 0:1, 1:-1, 1:-1].set(lower_x)
    weight_pad = weight_pad.at[1, 1:-1, 0:1, 1:-1].set(lower_y)
    weight_pad = weight_pad.at[2, 1:-1, 1:-1, 0:1].set(lower_z)
    weight_pad = jnp.repeat(weight_pad, BLOCK, axis=3)

    def apply_once(field):
        padded = with_halo(field, (("gx", 0), ("gy", 1), ("gz", 2)), 1)
        padded = padded.reshape(size_x + 2, size_y + 2, (size_z + 2) * BLOCK)
        return stencil(padded, weight_pad, shift_value, BLOCK).reshape(
            size_x, size_y, size_z, BLOCK
        )

    previous = start_block
    current = apply_once(start_block)
    powers = [current]
    for degree in range(1, POWERS):
        following = 2.0 * apply_once(current) - previous
        previous, current = (current, following)
        powers.append(following)
    krylov = jnp.stack(powers, axis=3).reshape(cell_local, BLOCK * POWERS)
    first_coef = (
        lax.psum(jnp.dot(basis_rows.T, krylov, precision=PRECISE), ("gx", "gy", "gz")) / cell_count
    )
    once = krylov - jnp.dot(basis_rows, first_coef, precision=PRECISE)
    second_coef = (
        lax.psum(jnp.dot(basis_rows.T, once, precision=PRECISE), ("gx", "gy", "gz")) / cell_count
    )
    twice = once - jnp.dot(basis_rows, second_coef, precision=PRECISE)
    gram_matrix = (
        lax.psum(jnp.dot(twice.T, twice, precision=PRECISE), ("gx", "gy", "gz")) / cell_count
    )
    lower_factor = jnp.linalg.cholesky(gram_matrix)
    solved = jax.scipy.linalg.solve_triangular(lower_factor, twice.T, lower=True)
    new_basis = solved.T.reshape(size_x, size_y, size_z * BLOCK * POWERS)
    return (new_basis, first_coef + second_coef, lower_factor.T)


def solution(mesh):
    return jax.shard_map(
        per_device,
        mesh=mesh,
        in_specs=(P("gx", "gy", "gz"), P(None, "gx", "gy", "gz"), P()),
        out_specs=(P("gx", "gy", "gz"), P(), P()),
        check_vma=False,
    )
```

profile of v0, /device:TPU:1, one launch (start us, length us, event | category | flops | bytes accessed | tf_op | source)
XLA Modules:
  0.0 644.6 jit_solution(5951552109017409170)
XLA Ops:
  8.5 4.5 collective-permute-start.3
  13.1 5.6 collective-permute-start.4
  19.6 3.7 collective-permute-start.5
  23.4 1.3 collective-permute-start.6
  24.7 2.1 collective-permute-start
  26.8 2.1 collective-permute-done.6
  28.9 3.2 collective-permute-start.7
  32.2 1.3 collective-permute-start.8
  33.6 4.0 collective-permute-start.2
  37.6 4.0 collective-permute-start.1
  44.4 2.5 broadcast_in_dim.5
  46.9 3.1 reshape.205
  50.7 1.3 pad_maximum_fusion.1
  52.9 4.1 collective-permute-start.9
  57.3 1.9 collective-permute-start.10
  59.3 4.3 collective-permute-done.10
  63.6 5.2 collective-permute-start.11
  68.8 1.3 collective-permute-start.12
  70.1 5.1 collective-permute-done.12
  75.4 3.2 collective-permute-start.13
  79.9 4.2 collective-permute-done.14
  85.6 4.5 collective-permute-start.15
  90.1 1.9 collective-permute-start.16
  92.1 4.3 collective-permute-done.16
  96.4 3.4 collective-permute-start.17
  101.2 3.6 collective-permute-done.18
  104.9 4.9 collective-permute-start.19
  109.8 1.3 collective-permute-start.20
  111.1 3.9 collective-permute-done.20
  117.0 4.8 collective-permute-start.21
  121.8 2.1 collective-permute-start.22
  123.9 4.3 collective-permute-done.22
  128.2 4.8 collective-permute-start.23
  133.0 1.3 collective-permute-start.24
  134.3 4.1 collective-permute-done.24
  139.2 4.3 collective-permute-start.25
  143.4 1.5 collective-permute-start.26
  145.3 1.9 mul.143
  147.2 2.0 sub.130
  149.2 2.2 pad_maximum_fusion.4
  151.4 1.7 reshape.211
  154.9 2.7 copy.16
  157.6 2.4 reshape.212
  161.2 95.3 %psum.21 = f32[96,128]{1,0:T(8,128)S(1)} all-reduce(f32[96,128]{1,0:T(8,128)S(1)} %convolution_bitcast_fusion.3), channel_id=1, replica_groups=mesh['gx'=8,'gy'=8,'gz'=8] {'gx','gy','gz'}, use_global_device_ids=true, to_apply=%region_0.1 | all-reduce | flops 12288 | bytes 98304 | tf_op jit(solution)/shard_map/psum | solution.py:97
  258.2 94.9 %psum.22 = f32[96,128]{1,0:T(8,128)S(1)} all-reduce(f32[96,128]{1,0:T(8,128)S(1)} %convolution_bitcast_fusion.2), channel_id=1, replica_groups=mesh['gx'=8,'gy'=8,'gz'=8] {'gx','gy','gz'}, use_global_device_ids=true, to_apply=%region_1.2 | all-reduce | flops 12288 | bytes 98304 | tf_op jit(solution)/shard_map/psum | solution.py:101
  355.6 254.9 %all-reduce.3.cloned.1.call-done = f32[128,128]{0,1:T(8,128)} async-done(((f32[128,128]{0,1:T(8,128)}), f32[128,128]{0,1:T(8,128)}) %all-reduce.3.cloned.1.call-update) | async-done | bytes 65552 | tf_op jit(solution)/shard_map/psum | solution.py:105
  612.3 11.7 %cholesky.16 = f32[128,128]{1,0:T(8,128)S(1)} custom-call(f32[128,128]{1,0:T(8,128)S(1)} %fusion.63), custom_call_target="Cholesky" | custom-call | tf_op jit(solution)/shard_map/jit(cholesky)/cholesky | solution.py:107
  625.4 9.8 %custom-call.7 = f32[1,128,128]{1,2,0:T(8,128)S(1)} custom-call(f32[1,128,128]{2,1,0:T(8,128)S(1)} %get-tuple-element.70), custom_call_target="InvertDiagBlocksLowerTriangular" | custom-call | tf_op jit(solution)/shard_map/jit(_solve_triangular)/triangular_solve | solution.py:108
  (116 shorter events, 26.8 us)
Async XLA Ops:
  7.2 603.3 %all-reduce.3.cloned.1.call-start = ((), (), s32[]{:S(2)}) async-start(), calls=%async_computation | async-start | bytes 131072 | tf_op jit(solution)/shard_map/psum | solution.py:105
  8.4 16.3 %copy-start.11 = (f32[3,4,16,16]{3,2,1,0:T(8,128)S(1)}, f32[3,4,16,16]{3,2,1,0:T(8,128)}, u32[]{:S(2)}) copy-start(f32[3,4,16,16]{3,2,1,0:T(8,128)} %param.10) | copy-start | bytes 36868
  8.5 10.3 %collective-permute-start.3 = (f32[1,16,16,32]{3,2,1,0:T(8,128)S(1)}, f32[1,16,16,32]{3,2,1,0:T(8,128)S(1)}, u32[]{:S(2)}, u32[]{:S(2)}) collective-permute-start(f32[1,16,16,32]{3,2,1,0:T(8,128)S(1)} %get-tuple-element.65), channel_id=1, source_target_pairs={{0,64},{64,128},{128,192},{192,256},{256,320},{320,384},{384,448},... | collective-permute-start | bytes 98312 | tf_op jit(solution)/shard_map/ppermute | solution.py:24
  13.1 6.5 %collective-permute-start.4 = (f32[1,16,16,32]{3,2,1,0:T(8,128)S(1)}, f32[1,16,16,32]{3,2,1,0:T(8,128)S(1)}, u32[]{:S(2)}, u32[]{:S(2)}) collective-permute-start(f32[1,16,16,32]{3,2,1,0:T(8,128)S(1)} %get-tuple-element.66), channel_id=1, source_target_pairs={{64,0},{128,64},{192,128},{256,192},{320,256},{384,320},{448,384},... | collective-permute-start | bytes 98312 | tf_op jit(solution)/shard_map/ppermute | solution.py:27
  18.8 25.6 %copy-start.6 = (f32[1,16,16,32]{3,2,1,0:T(8,128)}, f32[1,16,16,32]{3,2,1,0:T(8,128)S(1)}, u32[]{:S(2)}) copy-start(f32[1,16,16,32]{3,2,1,0:T(8,128)S(1)} %collective-permute-done.3) | copy-start | bytes 98308
  19.6 24.8 %copy-start.7 = (f32[1,16,16,32]{3,2,1,0:T(8,128)}, f32[1,16,16,32]{3,2,1,0:T(8,128)S(1)}, u32[]{:S(2)}) copy-start(f32[1,16,16,32]{3,2,1,0:T(8,128)S(1)} %collective-permute-done.4) | copy-start | bytes 98308
  19.6 7.1 %collective-permute-start.5 = (f32[6,1,16,32]{3,2,1,0:T(8,128)S(1)}, f32[6,1,16,32]{3,2,1,0:T(8,128)S(1)}, u32[]{:S(2)}, u32[]{:S(2)}) collective-permute-start(f32[6,1,16,32]{3,2,1,0:T(8,128)S(1)} %get-tuple-element.59), channel_id=1, source_target_pairs={{0,8},{8,16},{16,24},{24,32},{32,40},{40,48},{48,56},{1,9},{9,17},... | collective-permute-start | bytes 36872 | tf_op jit(solution)/shard_map/ppermute | solution.py:24
  23.4 5.5 collective-permute-start.6
  24.7 17.8 %collective-permute-start = (f32[1,16,16]{2,1,0:T(8,128)S(1)}, f32[1,16,16]{2,1,0:T(8,128)S(1)}, u32[]{:S(2)}, u32[]{:S(2)}) collective-permute-start(f32[1,16,16]{2,1,0:T(8,128)S(1)} %slice_bitcast_fusion.6), channel_id=1, source_target_pairs={{0,64},{64,128},{128,192},{192,256},{256,320},{320,384},{384,448},... | collective-permute-start | bytes 3080 | tf_op jit(solution)/shard_map/ppermute | solution.py:16
  28.8 8.8 %copy-start.12 = (f32[6,1,16,32]{3,2,1,0:T(8,128)}, f32[6,1,16,32]{3,2,1,0:T(8,128)S(1)}, u32[]{:S(2)}) copy-start(f32[6,1,16,32]{3,2,1,0:T(8,128)S(1)} %collective-permute-done.6) | copy-start | bytes 36868
  28.9 21.1 %collective-permute-start.7 = (f32[6,18,1,32]{3,2,1,0:T(1,128)S(1)}, f32[6,18,1,32]{3,2,1,0:T(1,128)S(1)}, u32[]{:S(2)}, u32[]{:S(2)}) collective-permute-start(f32[6,18,1,32]{3,2,1,0:T(1,128)S(1)} %get-tuple-element.51), channel_id=1, source_target_pairs={{0,1},{1,2},{2,3},{3,4},{4,5},{5,6},{6,7},{8,9},{9,10},{10,11},{11... | collective-permute-start | bytes 41480 | tf_op jit(solution)/shard_map/ppermute | solution.py:24
  32.2 18.5 %collective-permute-start.8 = (f32[6,18,1,32]{3,2,1,0:T(1,128)S(1)}, f32[6,18,1,32]{3,2,1,0:T(1,128)}, u32[]{:S(2)}, u32[]{:S(2)}) collective-permute-start(f32[6,18,1,32]{3,2,1,0:T(1,128)S(1)} %get-tuple-element.52), channel_id=1, source_target_pairs={{1,0},{2,1},{3,2},{4,3},{5,4},{6,5},{7,6},{9,8},{10,9},{11,10},{12... | collective-permute-start | bytes 41480 | tf_op jit(solution)/shard_map/ppermute | solution.py:27
  33.6 8.8 %collective-permute-start.2 = (f32[4,16,1]{1,0,2:T(4,128)S(1)}, f32[4,16,1]{1,0,2:T(4,128)S(1)}, u32[]{:S(2)}, u32[]{:S(2)}) collective-permute-start(f32[4,16,1]{1,0,2:T(4,128)S(1)} %bitcast.113), channel_id=1, source_target_pairs={{0,1},{1,2},{2,3},{3,4},{4,5},{5,6},{6,7},{8,9},{9,10},{10,11},{11... | collective-permute-start | bytes 776 | tf_op jit(solution)/shard_map/ppermute | solution.py:16
  37.6 5.7 collective-permute-start.1
  50.0 0.6 copy-start.15
  52.8 10.8 %copy-start.3 = (f32[4,16,512]{2,1,0:T(8,128)}, f32[4,16,512]{2,1,0:T(8,128)S(1)}, u32[]{:S(2)}) copy-start(f32[4,16,512]{2,1,0:T(8,128)S(1)} %fusion.51) | copy-start | bytes 393220
  52.9 6.3 collective-permute-start.9
  57.2 18.2 %copy-start = (f32[4,16,16,32]{3,2,1,0:T(8,128)}, f32[4,16,16,32]{3,2,1,0:T(8,128)S(1)}, u32[]{:S(2)}) copy-start(f32[4,16,16,32]{3,2,1,0:T(8,128)S(1)} %reshape.208) | copy-start | bytes 393220
  57.3 6.3 collective-permute-start.10
  63.6 6.5 %collective-permute-start.11 = (f32[6,1,16,32]{3,2,1,0:T(8,128)S(1)}, f32[6,1,16,32]{3,2,1,0:T(8,128)S(1)}, u32[]{:S(2)}, u32[]{:S(2)}) collective-permute-start(f32[6,1,16,32]{3,2,1,0:T(8,128)S(1)} %get-tuple-element.57), channel_id=1, source_target_pairs={{0,8},{8,16},{16,24},{24,32},{32,40},{40,48},{48,56},{1,9},{9,17},... | collective-permute-start | bytes 36872 | tf_op jit(solution)/shard_map/ppermute | solution.py:24
  68.8 6.4 %collective-permute-start.12 = (f32[6,1,16,32]{3,2,1,0:T(8,128)S(1)}, f32[6,1,16,32]{3,2,1,0:T(8,128)S(1)}, u32[]{:S(2)}, u32[]{:S(2)}) collective-permute-start(f32[6,1,16,32]{3,2,1,0:T(8,128)S(1)} %get-tuple-element.58), channel_id=1, source_target_pairs={{8,0},{16,8},{24,16},{32,24},{40,32},{48,40},{56,48},{9,1},{17,9},... | collective-permute-start | bytes 36872 | tf_op jit(solution)/shard_map/ppermute | solution.py:27
  75.4 4.5 collective-permute-start.13
  78.6 5.5 collective-permute-start.14
  85.6 6.4 collective-permute-start.15
  90.1 6.3 collective-permute-start.16
  96.4 4.7 collective-permute-start.17
  99.8 5.0 collective-permute-start.18
  104.9 6.2 collective-permute-start.19
  109.8 5.2 collective-permute-start.20
  115.6 1.3 copy-start.1
  116.1 0.7 copy-start.10
  117.0 27.9 %copy-start.5 = (f32[4,16,1536]{2,1,0:T(8,128)S(1)}, f32[4,16,1536]{2,1,0:T(8,128)}, u32[]{:S(2)}) copy-start(f32[4,16,1536]{2,1,0:T(8,128)} %param.9) | copy-start | bytes 1179652
  117.0 6.8 %collective-permute-start.21 = (f32[1,16,16,32]{3,2,1,0:T(8,128)S(1)}, f32[1,16,16,32]{3,2,1,0:T(8,128)S(1)}, u32[]{:S(2)}, u32[]{:S(2)}) collective-permute-start(f32[1,16,16,32]{3,2,1,0:T(8,128)S(1)} %get-tuple-element.61), channel_id=1, source_target_pairs={{0,64},{64,128},{128,192},{192,256},{256,320},{320,384},{384,448},... | collective-permute-start | bytes 98312 | tf_op jit(solution)/shard_map/ppermute | solution.py:24
  121.8 23.3 %copy-start.4 = (f32[4,16,512]{2,1,0:T(8,128)S(1)}, f32[4,16,512]{2,1,0:T(8,128)}, u32[]{:S(2)}) copy-start(f32[4,16,512]{2,1,0:T(8,128)} %copy-done.3) | copy-start | bytes 393220
  121.8 6.4 collective-permute-start.22
  128.2 16.7 %copy-start.8 = (f32[1,16,16,32]{3,2,1,0:T(8,128)}, f32[1,16,16,32]{3,2,1,0:T(8,128)S(1)}, u32[]{:S(2)}) copy-start(f32[1,16,16,32]{3,2,1,0:T(8,128)S(1)} %collective-permute-done.22) | copy-start | bytes 98308
  128.2 6.1 collective-permute-start.23
  133.0 5.4 collective-permute-start.24
  138.4 5.0 copy-start.13
  139.2 10.0 %collective-permute-start.25 = (f32[6,18,1,32]{3,2,1,0:T(1,128)}, f32[6,18,1,32]{3,2,1,0:T(1,128)}, u32[]{:S(2)}, u32[]{:S(2)}) collective-permute-start(f32[6,18,1,32]{3,2,1,0:T(1,128)} %get-tuple-element.45), channel_id=1, source_target_pairs={{0,1},{1,2},{2,3},{3,4},{4,5},{5,6},{6,7},{8,9},{9,10},{10,11},{11... | collective-permute-start | bytes 41480 | tf_op jit(solution)/shard_map/ppermute | solution.py:24
  143.4 5.7 collective-permute-start.26
  145.3 3.9 copy-start.9
  147.2 2.0 copy-start.14
  153.5 1.0 copy-start.2
Sparse Core Ops, SparseCore 0:
  355.1 255.3 all-reduce.2
where the time goes:
time: 646 us; the launch traced here: 645 us
  waiting for transfers between devices  292 us (45%)
  blocking collectives  190 us (29%)
  starting transfers between devices  82.5 us (13%)
  other arithmetic  34.8 us (5%)
  local copies, waits for them, and re-layouts  24.4 us (4%)
  between operations  15.5 us (2%)
    psum x1, waiting for transfers between devices, per_device(): lax.psum(jnp.dot(twice.T, twice, precision=PRECISE), ('gx', 'gy', 'gz'))  255 us
    psum x1, blocking collectives, per_device(): lax.psum(jnp.dot(basis_rows.T, krylov, precision=PRECISE), ('gx', 'gy', '...  95.3 us
    psum x1, blocking collectives, per_device(): lax.psum(jnp.dot(basis_rows.T, once, precision=PRECISE), ('gx', 'gy', 'gz'))  94.9 us
    ppermute x12, starting transfers between devices, with_halo(): lax.ppermute(lax.slice_in_dim(block, block.shape[dim] - width, None, axis...  50.5 us
    ppermute x12, waiting for transfers between devices, with_halo(): lax.ppermute(lax.slice_in_dim(block, 0, width, axis=dim), axis, backward)  36.7 us
    ppermute x12, starting transfers between devices, with_halo(): lax.ppermute(lax.slice_in_dim(block, 0, width, axis=dim), axis, backward)  22 us
  transfers between devices with their start and end apart: 28, of which 11 were waited for; matrix products, arithmetic and copies ran while one was open for 2% of the time, Pallas kernels for 0%

commit v1 on v0

--- a/solution.py
+++ b/solution.py
@@ -102,7 +102,8 @@
     )
     twice = once - jnp.dot(basis_rows, second_coef, precision=PRECISE)
     gram_matrix = (
-        lax.psum(jnp.dot(twice.T, twice, precision=PRECISE), ("gx", "gy", "gz")) / cell_count
+        lax.psum(lax.psum(jnp.dot(twice.T, twice, precision=PRECISE), "gx"), ("gy", "gz"))
+        / cell_count
     )
     lower_factor = jnp.linalg.cholesky(gram_matrix)
     solved = jax.scipy.linalg.solve_triangular(lower_factor, twice.T, lower=True)

time: 646 us -> 604 us (0.935)
  waiting for transfers between devices: 292 us -> 249 us
    psum x1 -> x2, waiting for transfers between devices: 255 us -> 212 us  [the longest x1 148 us: per_device(): lax.psum(lax.psum(jnp.dot(twice.T, twice, precision=PRECISE), 'gx'), ('gy...]
  transfers between devices with their start and end apart: 28 -> 29, of which waited for: 11 -> 12; matrix products, arithmetic and copies ran while one was open for 2% -> 2% of each run, Pallas kernels for 0% -> 0%
where the time goes in v1:
time: 604 us; the launch traced here: 599 us
  waiting for transfers between devices  249 us (41%)
  blocking collectives  190 us (31%)
  starting transfers between devices  82.8 us (14%)
  other arithmetic  34.8 us (6%)
  local copies, waits for them, and re-layouts  21.4 us (4%)
  between operations  15.5 us (3%)
    psum x1, waiting for transfers between devices, per_device(): lax.psum(lax.psum(jnp.dot(twice.T, twice, precision=PRECISE), 'gx'), ('gy...  148 us
    psum x1, blocking collectives, per_device(): lax.psum(jnp.dot(basis_rows.T, krylov, precision=PRECISE), ('gx', 'gy', '...  95.3 us
    psum x1, blocking collectives, per_device(): lax.psum(jnp.dot(basis_rows.T, once, precision=PRECISE), ('gx', 'gy', 'gz'))  94.7 us
    psum x1, waiting for transfers between devices, per_device(): lax.psum(jnp.dot(twice.T, twice, precision=PRECISE), 'gx')  64 us
    ppermute x12, starting transfers between devices, with_halo(): lax.ppermute(lax.slice_in_dim(block, block.shape[dim] - width, None, axis...  50.5 us
    ppermute x12, waiting for transfers between devices, with_halo(): lax.ppermute(lax.slice_in_dim(block, 0, width, axis=dim), axis, backward)  36.8 us
    ppermute x12, starting transfers between devices, with_halo(): lax.ppermute(lax.slice_in_dim(block, 0, width, axis=dim), axis, backward)  22 us
    another operation x3, other arithmetic, per_device(): lower_factor = jnp.linalg.cholesky(gram_matrix)  12.4 us
  transfers between devices with their start and end apart: 29, of which 12 were waited for; matrix products, arithmetic and copies ran while one was open for 2% of the time, Pallas kernels for 0%

profile of v1, /device:TPU:1, one launch (start us, length us, event | category | flops | bytes accessed | tf_op | source)
XLA Modules:
  0.0 598.5 jit_solution(11768620580181454831)
XLA Ops:
  8.5 4.5 collective-permute-start.3
  13.1 5.6 collective-permute-start.4
  19.6 3.7 collective-permute-start.5
  23.4 1.3 collective-permute-start.6
  24.7 2.1 collective-permute-start
  26.8 2.1 collective-permute-done.6
  29.0 3.2 collective-permute-start.7
  32.2 1.3 collective-permute-start.8
  33.6 4.0 collective-permute-start.2
  37.6 4.0 collective-permute-start.1
  44.4 2.5 broadcast_in_dim.5
  46.9 3.1 reshape.205
  50.7 1.3 pad_maximum_fusion.1
  52.9 4.1 collective-permute-start.9
  57.3 1.9 collective-permute-start.10
  59.3 4.3 collective-permute-done.10
  63.6 5.2 collective-permute-start.11
  68.8 1.3 collective-permute-start.12
  70.1 5.1 collective-permute-done.12
  75.4 3.2 collective-permute-start.13
  79.9 4.2 collective-permute-done.14
  85.6 4.5 collective-permute-start.15
  90.1 1.9 collective-permute-start.16
  92.1 4.3 collective-permute-done.16
  96.4 3.4 collective-permute-start.17
  99.9 1.3 collective-permute-start.18
  101.2 3.7 collective-permute-done.18
  104.9 4.9 collective-permute-start.19
  109.8 1.3 collective-permute-start.20
  111.1 3.9 collective-permute-done.20
  117.0 4.7 collective-permute-start.21
  121.8 2.1 collective-permute-start.22
  123.9 4.3 collective-permute-done.22
  128.2 4.8 collective-permute-start.23
  134.3 4.1 collective-permute-done.24
  139.2 4.3 collective-permute-start.25
  143.4 1.5 collective-permute-start.26
  145.3 1.9 mul.143
  147.2 1.9 sub.130
  149.1 2.2 pad_maximum_fusion.4
  151.4 1.7 reshape.211
  154.8 1.4 copy.16
  158.3 95.3 %psum.28 = f32[96,128]{1,0:T(8,128)S(1)} all-reduce(f32[96,128]{1,0:T(8,128)S(1)} %convolution_bitcast_fusion.3), channel_id=1, replica_groups=mesh['gx'=8,'gy'=8,'gz'=8] {'gx','gy','gz'}, use_global_device_ids=true, to_apply=%region_0.1 | all-reduce | flops 12288 | bytes 98304 | tf_op jit(solution)/shard_map/psum | solution.py:97
  255.2 94.7 %psum.29 = f32[96,128]{1,0:T(8,128)S(1)} all-reduce(f32[96,128]{1,0:T(8,128)S(1)} %convolution_bitcast_fusion.2), channel_id=1, replica_groups=mesh['gx'=8,'gy'=8,'gz'=8] {'gx','gy','gz'}, use_global_device_ids=true, to_apply=%region_1.2 | all-reduce | flops 12288 | bytes 98304 | tf_op jit(solution)/shard_map/psum | solution.py:101
  352.1 64.0 %all-reduce.4.cloned.1.call-done = f32[128,128]{0,1:T(8,128)} async-done(((f32[128,128]{0,1:T(8,128)}), f32[128,128]{0,1:T(8,128)}) %all-reduce.4.cloned.1.call-update) | async-done | bytes 65552 | tf_op jit(solution)/shard_map/psum | solution.py:105
  416.8 147.6 %all-reduce.6.cloned.1.call-done = f32[128,128]{0,1:T(8,128)} async-done(((f32[128,128]{0,1:T(8,128)}), f32[128,128]{0,1:T(8,128)}) %all-reduce.6.cloned.1.call-update) | async-done | bytes 65552 | tf_op jit(solution)/shard_map/psum | solution.py:105
  566.2 11.7 %cholesky.16 = f32[128,128]{1,0:T(8,128)S(1)} custom-call(f32[128,128]{1,0:T(8,128)S(1)} %fusion.63), custom_call_target="Cholesky" | custom-call | tf_op jit(solution)/shard_map/jit(cholesky)/cholesky | solution.py:108
  579.3 9.8 %custom-call.7 = f32[1,128,128]{1,2,0:T(8,128)S(1)} custom-call(f32[1,128,128]{2,1,0:T(8,128)S(1)} %get-tuple-element.70), custom_call_target="InvertDiagBlocksLowerTriangular" | custom-call | tf_op jit(solution)/shard_map/jit(_solve_triangular)/triangular_solve | solution.py:109
  (119 shorter events, 28.0 us)
Async XLA Ops:
  7.2 409.0 %all-reduce.4.cloned.1.call-start = ((), (), s32[]{:S(2)}) async-start(), calls=%async_computation | async-start | bytes 131072 | tf_op jit(solution)/shard_map/psum | solution.py:105
  8.4 16.3 %copy-start.11 = (f32[3,4,16,16]{3,2,1,0:T(8,128)S(1)}, f32[3,4,16,16]{3,2,1,0:T(8,128)}, u32[]{:S(2)}) copy-start(f32[3,4,16,16]{3,2,1,0:T(8,128)} %param.10) | copy-start | bytes 36868
  8.5 10.3 %collective-permute-start.3 = (f32[1,16,16,32]{3,2,1,0:T(8,128)S(1)}, f32[1,16,16,32]{3,2,1,0:T(8,128)S(1)}, u32[]{:S(2)}, u32[]{:S(2)}) collective-permute-start(f32[1,16,16,32]{3,2,1,0:T(8,128)S(1)} %get-tuple-element.65), channel_id=1, source_target_pairs={{0,64},{64,128},{128,192},{192,256},{256,320},{320,384},{384,448},... | collective-permute-start | bytes 98312 | tf_op jit(solution)/shard_map/ppermute | solution.py:24
  13.1 6.5 %collective-permute-start.4 = (f32[1,16,16,32]{3,2,1,0:T(8,128)S(1)}, f32[1,16,16,32]{3,2,1,0:T(8,128)S(1)}, u32[]{:S(2)}, u32[]{:S(2)}) collective-permute-start(f32[1,16,16,32]{3,2,1,0:T(8,128)S(1)} %get-tuple-element.66), channel_id=1, source_target_pairs={{64,0},{128,64},{192,128},{256,192},{320,256},{384,320},{448,384},... | collective-permute-start | bytes 98312 | tf_op jit(solution)/shard_map/ppermute | solution.py:27
  18.8 10.0 %copy-start.6 = (f32[1,16,16,32]{3,2,1,0:T(8,128)}, f32[1,16,16,32]{3,2,1,0:T(8,128)S(1)}, u32[]{:S(2)}) copy-start(f32[1,16,16,32]{3,2,1,0:T(8,128)S(1)} %collective-permute-done.3) | copy-start | bytes 98308
  19.6 9.4 %copy-start.7 = (f32[1,16,16,32]{3,2,1,0:T(8,128)}, f32[1,16,16,32]{3,2,1,0:T(8,128)S(1)}, u32[]{:S(2)}) copy-start(f32[1,16,16,32]{3,2,1,0:T(8,128)S(1)} %collective-permute-done.4) | copy-start | bytes 98308
  19.6 7.1 %collective-permute-start.5 = (f32[6,1,16,32]{3,2,1,0:T(8,128)S(1)}, f32[6,1,16,32]{3,2,1,0:T(8,128)S(1)}, u32[]{:S(2)}, u32[]{:S(2)}) collective-permute-start(f32[6,1,16,32]{3,2,1,0:T(8,128)S(1)} %get-tuple-element.59), channel_id=1, source_target_pairs={{0,8},{8,16},{16,24},{24,32},{32,40},{40,48},{48,56},{1,9},{9,17},... | collective-permute-start | bytes 36872 | tf_op jit(solution)/shard_map/ppermute | solution.py:24
  23.4 5.5 collective-permute-start.6
  24.7 17.8 %collective-permute-start = (f32[1,16,16]{2,1,0:T(8,128)S(1)}, f32[1,16,16]{2,1,0:T(8,128)S(1)}, u32[]{:S(2)}, u32[]{:S(2)}) collective-permute-start(f32[1,16,16]{2,1,0:T(8,128)S(1)} %slice_bitcast_fusion.6), channel_id=1, source_target_pairs={{0,64},{64,128},{128,192},{192,256},{256,320},{320,384},{384,448},... | collective-permute-start | bytes 3080 | tf_op jit(solution)/shard_map/ppermute | solution.py:16
  28.8 15.6 %copy-start.12 = (f32[6,1,16,32]{3,2,1,0:T(8,128)}, f32[6,1,16,32]{3,2,1,0:T(8,128)S(1)}, u32[]{:S(2)}) copy-start(f32[6,1,16,32]{3,2,1,0:T(8,128)S(1)} %collective-permute-done.6) | copy-start | bytes 36868
  29.0 21.1 %collective-permute-start.7 = (f32[6,18,1,32]{3,2,1,0:T(1,128)S(1)}, f32[6,18,1,32]{3,2,1,0:T(1,128)S(1)}, u32[]{:S(2)}, u32[]{:S(2)}) collective-permute-start(f32[6,18,1,32]{3,2,1,0:T(1,128)S(1)} %get-tuple-element.51), channel_id=1, source_target_pairs={{0,1},{1,2},{2,3},{3,4},{4,5},{5,6},{6,7},{8,9},{9,10},{10,11},{11... | collective-permute-start | bytes 41480 | tf_op jit(solution)/shard_map/ppermute | solution.py:24
  32.2 18.5 %collective-permute-start.8 = (f32[6,18,1,32]{3,2,1,0:T(1,128)S(1)}, f32[6,18,1,32]{3,2,1,0:T(1,128)}, u32[]{:S(2)}, u32[]{:S(2)}) collective-permute-start(f32[6,18,1,32]{3,2,1,0:T(1,128)S(1)} %get-tuple-element.52), channel_id=1, source_target_pairs={{1,0},{2,1},{3,2},{4,3},{5,4},{6,5},{7,6},{9,8},{10,9},{11,10},{12... | collective-permute-start | bytes 41480 | tf_op jit(solution)/shard_map/ppermute | solution.py:27
  33.6 8.8 %collective-permute-start.2 = (f32[4,16,1]{1,0,2:T(4,128)S(1)}, f32[4,16,1]{1,0,2:T(4,128)S(1)}, u32[]{:S(2)}, u32[]{:S(2)}) collective-permute-start(f32[4,16,1]{1,0,2:T(4,128)S(1)} %bitcast.113), channel_id=1, source_target_pairs={{0,1},{1,2},{2,3},{3,4},{4,5},{5,6},{6,7},{8,9},{9,10},{10,11},{11... | collective-permute-start | bytes 776 | tf_op jit(solution)/shard_map/ppermute | solution.py:16
  37.6 5.7 collective-permute-start.1
  50.0 0.6 copy-start.15
  52.8 10.8 %copy-start.3 = (f32[4,16,512]{2,1,0:T(8,128)}, f32[4,16,512]{2,1,0:T(8,128)S(1)}, u32[]{:S(2)}) copy-start(f32[4,16,512]{2,1,0:T(8,128)S(1)} %fusion.51) | copy-start | bytes 393220
  52.9 6.3 %collective-permute-start.9 = (f32[1,16,16,32]{3,2,1,0:T(8,128)S(1)}, f32[1,16,16,32]{3,2,1,0:T(8,128)S(1)}, u32[]{:S(2)}, u32[]{:S(2)}) collective-permute-start(f32[1,16,16,32]{3,2,1,0:T(8,128)S(1)} %slice.363), channel_id=1, source_target_pairs={{0,64},{64,128},{128,192},{192,256},{256,320},{320,384},{384,448},... | collective-permute-start | bytes 98312 | tf_op jit(solution)/shard_map/ppermute | solution.py:24
  57.2 18.2 %copy-start = (f32[4,16,16,32]{3,2,1,0:T(8,128)}, f32[4,16,16,32]{3,2,1,0:T(8,128)S(1)}, u32[]{:S(2)}) copy-start(f32[4,16,16,32]{3,2,1,0:T(8,128)S(1)} %reshape.208) | copy-start | bytes 393220
  57.3 6.3 %collective-permute-start.10 = (f32[1,16,16,32]{3,2,1,0:T(8,128)S(1)}, f32[1,16,16,32]{3,2,1,0:T(8,128)S(1)}, u32[]{:S(2)}, u32[]{:S(2)}) collective-permute-start(f32[1,16,16,32]{3,2,1,0:T(8,128)S(1)} %slice.365), channel_id=1, source_target_pairs={{64,0},{128,64},{192,128},{256,192},{320,256},{384,320},{448,384},... | collective-permute-start | bytes 98312 | tf_op jit(solution)/shard_map/ppermute | solution.py:27
  63.6 6.5 %collective-permute-start.11 = (f32[6,1,16,32]{3,2,1,0:T(8,128)S(1)}, f32[6,1,16,32]{3,2,1,0:T(8,128)S(1)}, u32[]{:S(2)}, u32[]{:S(2)}) collective-permute-start(f32[6,1,16,32]{3,2,1,0:T(8,128)S(1)} %get-tuple-element.57), channel_id=1, source_target_pairs={{0,8},{8,16},{16,24},{24,32},{32,40},{40,48},{48,56},{1,9},{9,17},... | collective-permute-start | bytes 36872 | tf_op jit(solution)/shard_map/ppermute | solution.py:24
  68.8 6.4 %collective-permute-start.12 = (f32[6,1,16,32]{3,2,1,0:T(8,128)S(1)}, f32[6,1,16,32]{3,2,1,0:T(8,128)S(1)}, u32[]{:S(2)}, u32[]{:S(2)}) collective-permute-start(f32[6,1,16,32]{3,2,1,0:T(8,128)S(1)} %get-tuple-element.58), channel_id=1, source_target_pairs={{8,0},{16,8},{24,16},{32,24},{40,32},{48,40},{56,48},{9,1},{17,9},... | collective-permute-start | bytes 36872 | tf_op jit(solution)/shard_map/ppermute | solution.py:27
  75.4 4.5 collective-permute-start.13
  78.6 5.5 collective-permute-start.14
  85.6 6.4 %collective-permute-start.15 = (f32[1,16,16,32]{3,2,1,0:T(8,128)S(1)}, f32[1,16,16,32]{3,2,1,0:T(8,128)S(1)}, u32[]{:S(2)}, u32[]{:S(2)}) collective-permute-start(f32[1,16,16,32]{3,2,1,0:T(8,128)S(1)} %get-tuple-element.63), channel_id=1, source_target_pairs={{0,64},{64,128},{128,192},{192,256},{256,320},{320,384},{384,448},... | collective-permute-start | bytes 98312 | tf_op jit(solution)/shard_map/ppermute | solution.py:24
  90.1 6.3 %collective-permute-start.16 = (f32[1,16,16,32]{3,2,1,0:T(8,128)S(1)}, f32[1,16,16,32]{3,2,1,0:T(8,128)S(1)}, u32[]{:S(2)}, u32[]{:S(2)}) collective-permute-start(f32[1,16,16,32]{3,2,1,0:T(8,128)S(1)} %get-tuple-element.64), channel_id=1, source_target_pairs={{64,0},{128,64},{192,128},{256,192},{320,256},{384,320},{448,384},... | collective-permute-start | bytes 98312 | tf_op jit(solution)/shard_map/ppermute | solution.py:27
  96.4 4.7 collective-permute-start.17
  99.9 5.0 collective-permute-start.18
  104.9 6.2 %collective-permute-start.19 = (f32[6,18,1,32]{3,2,1,0:T(1,128)S(1)}, f32[6,18,1,32]{3,2,1,0:T(1,128)S(1)}, u32[]{:S(2)}, u32[]{:S(2)}) collective-permute-start(f32[6,18,1,32]{3,2,1,0:T(1,128)S(1)} %get-tuple-element.47), channel_id=1, source_target_pairs={{0,1},{1,2},{2,3},{3,4},{4,5},{5,6},{6,7},{8,9},{9,10},{10,11},{11... | collective-permute-start | bytes 41480 | tf_op jit(solution)/shard_map/ppermute | solution.py:24
  109.8 5.2 collective-permute-start.20
  115.6 1.3 copy-start.1
  116.1 0.7 copy-start.10
  117.0 27.9 %copy-start.5 = (f32[4,16,1536]{2,1,0:T(8,128)S(1)}, f32[4,16,1536]{2,1,0:T(8,128)}, u32[]{:S(2)}) copy-start(f32[4,16,1536]{2,1,0:T(8,128)} %param.9) | copy-start | bytes 1179652
  117.0 6.8 %collective-permute-start.21 = (f32[1,16,16,32]{3,2,1,0:T(8,128)S(1)}, f32[1,16,16,32]{3,2,1,0:T(8,128)S(1)}, u32[]{:S(2)}, u32[]{:S(2)}) collective-permute-start(f32[1,16,16,32]{3,2,1,0:T(8,128)S(1)} %get-tuple-element.61), channel_id=1, source_target_pairs={{0,64},{64,128},{128,192},{192,256},{256,320},{320,384},{384,448},... | collective-permute-start | bytes 98312 | tf_op jit(solution)/shard_map/ppermute | solution.py:24
  121.8 23.3 %copy-start.4 = (f32[4,16,512]{2,1,0:T(8,128)S(1)}, f32[4,16,512]{2,1,0:T(8,128)}, u32[]{:S(2)}) copy-start(f32[4,16,512]{2,1,0:T(8,128)} %copy-done.3) | copy-start | bytes 393220
  121.8 6.4 %collective-permute-start.22 = (f32[1,16,16,32]{3,2,1,0:T(8,128)S(1)}, f32[1,16,16,32]{3,2,1,0:T(8,128)S(1)}, u32[]{:S(2)}, u32[]{:S(2)}) collective-permute-start(f32[1,16,16,32]{3,2,1,0:T(8,128)S(1)} %get-tuple-element.62), channel_id=1, source_target_pairs={{64,0},{128,64},{192,128},{256,192},{320,256},{384,320},{448,384},... | collective-permute-start | bytes 98312 | tf_op jit(solution)/shard_map/ppermute | solution.py:27
  128.2 16.7 %copy-start.8 = (f32[1,16,16,32]{3,2,1,0:T(8,128)}, f32[1,16,16,32]{3,2,1,0:T(8,128)S(1)}, u32[]{:S(2)}) copy-start(f32[1,16,16,32]{3,2,1,0:T(8,128)S(1)} %collective-permute-done.22) | copy-start | bytes 98308
  128.2 6.1 %collective-permute-start.23 = (f32[6,1,16,32]{3,2,1,0:T(8,128)S(1)}, f32[6,1,16,32]{3,2,1,0:T(8,128)S(1)}, u32[]{:S(2)}, u32[]{:S(2)}) collective-permute-start(f32[6,1,16,32]{3,2,1,0:T(8,128)S(1)} %get-tuple-element.53), channel_id=1, source_target_pairs={{0,8},{8,16},{16,24},{24,32},{32,40},{40,48},{48,56},{1,9},{9,17},... | collective-permute-start | bytes 36872 | tf_op jit(solution)/shard_map/ppermute | solution.py:24
  133.0 5.4 collective-permute-start.24
  138.4 5.0 copy-start.13
  139.2 10.0 %collective-permute-start.25 = (f32[6,18,1,32]{3,2,1,0:T(1,128)}, f32[6,18,1,32]{3,2,1,0:T(1,128)}, u32[]{:S(2)}, u32[]{:S(2)}) collective-permute-start(f32[6,18,1,32]{3,2,1,0:T(1,128)} %get-tuple-element.45), channel_id=1, source_target_pairs={{0,1},{1,2},{2,3},{3,4},{4,5},{5,6},{6,7},{8,9},{9,10},{10,11},{11... | collective-permute-start | bytes 41480 | tf_op jit(solution)/shard_map/ppermute | solution.py:24
  143.4 5.7 collective-permute-start.26
  145.3 3.9 copy-start.9
  147.2 2.0 copy-start.14
  153.5 1.0 copy-start.2
  351.8 212.6 %all-reduce.6.cloned.1.call-start = ((), (), s32[]{:S(2)}) async-start(), calls=%async_computation.1 | async-start | bytes 131072 | tf_op jit(solution)/shard_map/psum | solution.py:105
Sparse Core Ops, SparseCore 0:
  351.9 64.1 all-reduce.3
  419.7 144.6 all-reduce.5
